TPU v7x, 512 devices: a whole 4x8x8 slice. The times are simulated.
512 devices in a mesh: grp: 8 (over y), row: 8 (over z), col: 8 (over x, core).
Axes of the slice: x: 4, y: 8, z: 8, core: 2. Of those that a mesh axis runs over, the one named last changes fastest.
Arguments:
- new_rows: bfloat16 [768, 16, 8192], P(('grp', 'col'), None, 'row'), may hold values from -6 to 6
- query_weight: bfloat16 [8192, 8192], P('row', 'col')
- key_weight: bfloat16 [8192, 1024], P('row', 'col')
- value_weight: bfloat16 [8192, 1024], P('row', 'col'), may hold values from -0.0625 to 0.0625
- cache_keys: bfloat16 [768, 512, 1024], P(('grp', 'row'), None, 'col'), may hold values from -6 to 6
- cache_values: bfloat16 [768, 512, 1024], P(('grp', 'row'), None, 'col'), may hold values from -6 to 6
- region_agents: int32 [768], replicated, may hold values from 0 to 767, as said below
- new_counts: int32 [768], replicated, may hold values from 4 to 16, as said below
- cache_lengths: int32 [768], replicated, may hold values from 1 to 512, as said below
Outputs:
- attended: bfloat16 [768, 16, 8192], P(('grp', 'col'), 'row')
Inputs may be any that keep to these rules, and one draw needn't show every extreme that they name: `region_agents`: A permutation of the 768 agents. Rows i with equal i // 12 form one region; agent a is served by group a // 96. Every region holds at most 3 agents served by one group, and exactly 3 of some group. `new_counts`: some agent has 16 new tokens. `cache_lengths`: some agent has 512 cached positions.
All inputs are finite; a program needn't handle non-finite values.
Results may differ from a plain program's by a relative error of at most 0.025.
Values may be sent and summed in bfloat16 or wider, within the bound.
A program may use at most 64 MiB of HBM per device.

v0:
```python
import jax
import jax.numpy as jnp
from jax import lax
from jax.sharding import PartitionSpec as P

HEAD_DIM = 128
rotary_base = 500000.0
floor_score = -1e30


def rotate_pairs(values, positions):
    half_dim = values.shape[-1] // 2
    exponent = jnp.arange(half_dim, dtype=jnp.float32) * (2.0 / values.shape[-1])
    frequency = rotary_base ** (-exponent)
    angles = positions.astype(jnp.float32)[..., None, None] * frequency
    cosine = jnp.cos(angles)
    sine_part = jnp.sin(angles)
    first_half = values[..., :half_dim]
    second = values[..., half_dim:]
    return jnp.concatenate(
        [first_half * cosine - second * sine_part, second * cosine + first_half * sine_part],
        axis=-1,
    )


def local(
    new_rows,
    query_weight,
    key_weight,
    value_weight,
    cache_keys,
    cache_values,
    region_agents,
    new_counts,
    cache_lengths,
):
    groups = lax.axis_size("grp")
    grid_rows = lax.axis_size("row")
    grid_cols = lax.axis_size("col")
    group_index = lax.axis_index("grp")
    row_index = lax.axis_index("row")
    col_index = lax.axis_index("col")
    agents_total = region_agents.shape[0]
    per_group = agents_total // groups
    per_region = new_rows.shape[0]
    regions = groups * grid_cols
    capacity = max(2, 2 * per_region // groups)
    slot_count = new_rows.shape[1]
    feature_width = new_rows.shape[2]
    slot_width = slot_count // grid_cols
    served_by = region_agents // per_group
    grouped = served_by.reshape(regions, per_region)
    earlier = jnp.arange(per_region)[:, None] > jnp.arange(per_region)[None, :]
    same_group = grouped[:, :, None] == grouped[:, None, :]
    bucket = jnp.sum((same_group & earlier[None, :, :]).astype(jnp.int32), axis=2).reshape(
        agents_total
    )
    slot_of_agent = jnp.argsort(region_agents)
    my_region = group_index * grid_cols + col_index
    mine_group = lax.dynamic_slice_in_dim(served_by, my_region * per_region, per_region)
    mine_bucket = lax.dynamic_slice_in_dim(bucket, my_region * per_region, per_region)
    choose = (
        (mine_group[None, None, :] == jnp.arange(groups)[:, None, None])
        & (mine_bucket[None, None, :] == jnp.arange(capacity)[None, :, None])
    ).astype(jnp.bfloat16)
    pieces = new_rows.reshape(per_region, grid_cols, slot_width, feature_width)
    outgoing = jnp.einsum(
        "gkj,jcsd->gcksd", choose, pieces, preferred_element_type=jnp.float32
    ).astype(jnp.bfloat16)
    arrived = lax.all_to_all(
        outgoing.reshape(regions, capacity, slot_width, feature_width),
        ("grp", "col"),
        split_axis=0,
        concat_axis=0,
        tiled=True,
    )
    my_slots = lax.dynamic_slice_in_dim(slot_of_agent, group_index * per_group, per_group)
    source_row = my_slots // per_region * capacity + jnp.take(bucket, my_slots)
    landed = jnp.take(
        arrived.reshape(regions * capacity, slot_width, feature_width), source_row, axis=0
    )
    tokens = lax.all_gather(landed, "col", axis=1, tiled=True)
    agents_here = cache_keys.shape[0]
    picked = tokens.reshape(lax.axis_size("row") * agents_here * slot_count, feature_width)
    query_part = jnp.dot(picked, query_weight, preferred_element_type=jnp.float32)
    key_part = jnp.dot(picked, key_weight, preferred_element_type=jnp.float32)
    value_part = jnp.dot(picked, value_weight, preferred_element_type=jnp.float32)
    summed = lax.psum_scatter(
        jnp.concatenate([query_part, key_part, value_part], axis=1)
        .reshape(lax.axis_size("row") * agents_here, slot_count, -1)
        .astype(jnp.bfloat16),
        "row",
        scatter_dimension=0,
        tiled=True,
    ).astype(jnp.float32)
    local_agents = (
        group_index * per_group + row_index * agents_here + jnp.arange(agents_here, dtype=jnp.int32)
    )
    lengths_now = jnp.take(cache_lengths, local_agents)
    counts_now = jnp.take(new_counts, local_agents)
    positions = lengths_now[:, None] + jnp.arange(slot_count, dtype=jnp.int32)[None, :]
    query_width = query_weight.shape[1]
    key_width = key_weight.shape[1]
    heads_here = query_width // HEAD_DIM
    kv_here = key_width // HEAD_DIM
    group_ratio = heads_here // kv_here
    queries = rotate_pairs(
        summed[:, :, :query_width].reshape(agents_here, slot_count, heads_here, HEAD_DIM), positions
    ).astype(jnp.bfloat16)
    fresh_keys = rotate_pairs(
        summed[:, :, query_width : query_width + key_width].reshape(
            agents_here, slot_count, kv_here, HEAD_DIM
        ),
        positions,
    ).astype(jnp.bfloat16)
    fresh_values = (
        summed[:, :, query_width + key_width :]
        .reshape(agents_here, slot_count, kv_here, HEAD_DIM)
        .astype(jnp.bfloat16)
    )
    query_rows = (
        queries.reshape(agents_here, slot_count, kv_here, group_ratio, HEAD_DIM)
        .transpose(0, 2, 3, 1, 4)
        .reshape(agents_here, kv_here, group_ratio * slot_count, HEAD_DIM)
    )
    cache_span = cache_keys.shape[1]
    stored_keys = cache_keys.reshape(agents_here, cache_span, kv_here, HEAD_DIM)
    stored_values = cache_values.reshape(agents_here, cache_span, kv_here, HEAD_DIM)
    score_scale = HEAD_DIM ** (-0.5)
    slot_of_row = jnp.arange(group_ratio * slot_count, dtype=jnp.int32) % slot_count
    fresh_index = jnp.arange(slot_count, dtype=jnp.int32)
    new_allowed = (
        (fresh_index[None, :] <= slot_of_row[:, None])[None, :, :]
        & (fresh_index[None, None, :] < counts_now[:, None, None])
    )[:, None, :, :]
    new_scores = (
        jnp.einsum("akrd,atkd->akrt", query_rows, fresh_keys, preferred_element_type=jnp.float32)
        * score_scale
    )
    cache_scores = (
        jnp.einsum("akrd,apkd->akrp", query_rows, stored_keys, preferred_element_type=jnp.float32)
        * score_scale
    )
    cache_allowed = (jnp.arange(cache_span, dtype=jnp.int32)[None, :] < lengths_now[:, None])[
        :, None, None, :
    ]
    cache_masked = jnp.where(cache_allowed, cache_scores, floor_score)
    new_masked = jnp.where(new_allowed, new_scores, floor_score)
    row_max = jnp.maximum(jnp.max(cache_masked, axis=3), jnp.max(new_masked, axis=3))
    cache_weights = jnp.where(cache_allowed, jnp.exp(cache_masked - row_max[..., None]), 0.0)
    new_weights = jnp.where(new_allowed, jnp.exp(new_masked - row_max[..., None]), 0.0)
    denominator = jnp.sum(cache_weights, axis=3) + jnp.sum(new_weights, axis=3)
    weighted = jnp.einsum(
        "akrp,apkd->akrd",
        cache_weights.astype(jnp.bfloat16),
        stored_values,
        preferred_element_type=jnp.float32,
    )
    weighted = weighted + jnp.einsum(
        "akrp,apkd->akrd",
        new_weights.astype(jnp.bfloat16),
        fresh_values,
        preferred_element_type=jnp.float32,
    )
    result = (
        (weighted / denominator[..., None])
        .reshape(agents_here, kv_here, group_ratio, slot_count, HEAD_DIM)
        .transpose(0, 3, 1, 2, 4)
        .reshape(agents_here, slot_count, query_width)
    )
    valid_slot = jnp.arange(slot_count, dtype=jnp.int32)[None, :] < counts_now[:, None]
    result = jnp.where(valid_slot[:, :, None], result, 0.0).astype(jnp.bfloat16)
    regrouped = lax.all_to_all(result, "row", split_axis=1, concat_axis=0, tiled=True)
    slot_share = slot_count // grid_rows
    choose_back = (
        jnp.arange(regions * capacity, dtype=jnp.int32)[:, None] == source_row[None, :]
    ).astype(jnp.bfloat16)
    returning = jnp.einsum(
        "qt,tsf->qsf", choose_back, regrouped, preferred_element_type=jnp.float32
    ).astype(jnp.bfloat16)
    incoming = lax.all_to_all(
        returning.reshape(regions, capacity, slot_share, query_width),
        ("grp", "col"),
        split_axis=0,
        concat_axis=0,
        tiled=True,
    ).reshape(groups, grid_cols, capacity, slot_share, query_width)
    select_back = (
        (mine_group[:, None, None] == jnp.arange(groups)[None, :, None])
        & (mine_bucket[:, None, None] == jnp.arange(capacity)[None, None, :])
    ).astype(jnp.bfloat16)
    finished = jnp.einsum(
        "jgk,gcksf->jscf", select_back, incoming, preferred_element_type=jnp.float32
    ).astype(jnp.bfloat16)
    return finished.reshape(per_region, slot_share, grid_cols * query_width)


def solution(mesh):
    placed = (
        P(("grp", "col"), None, "row"),
        P("row", "col"),
        P("row", "col"),
        P("row", "col"),
        P(("grp", "row"), None, "col"),
        P(("grp", "row"), None, "col"),
        P(),
        P(),
        P(),
    )
    return jax.shard_map(
        local, mesh=mesh, in_specs=placed, out_specs=P(("grp", "col"), "row", None), check_vma=False
    )
```

profile of v0, /device:TPU:1, one launch (start us, length us, event | category | flops | bytes accessed | tf_op | source)
XLA Modules:
  0.0 230.3 jit_solution(6798773412891268803)
XLA Ops:
  6.5 0.8 add_select_fusion
  8.1 1.2 copy.95
  10.1 1.7 copy.77
  11.8 11.6 %all-to-all-start = ((bf16[64,3,2,1024]{3,2,1,0:T(2,128)(2,1)}), bf16[64,3,2,1024]{3,2,1,0:T(2,128)(2,1)S(1)}, u32[]{:S(2)}, u32[]{:S(2)}) async-start(bf16[64,3,2,1024]{3,2,1,0:T(2,128)(2,1)} %copy.77), calls=%async_computation | async-start | bytes 1572864 | tf_op jit(solution)/shard_map/all_to_all | solution.py:70
  23.5 4.4 %sort.17 = (s32[768]{0:T(1024)}, s32[768]{0:T(1024)S(1)}) sort(s32[768]{0:T(1024)S(1)} %copy-done.7, s32[768]{0:T(1024)S(1)} %iota.103), dimensions={0}, to_apply=%region_0.1 | sort | flops 7680 | bytes 12288 | tf_op jit(solution)/shard_map/jit(argsort)/sort | solution.py:58
  27.9 1.0 gather_fusion
  29.0 17.1 %all-to-all-done = bf16[64,3,2,1024]{3,2,1,0:T(2,128)(2,1)S(1)} async-done(((bf16[64,3,2,1024]{3,2,1,0:T(2,128)(2,1)}), bf16[64,3,2,1024]{3,2,1,0:T(2,128)(2,1)S(1)}, u32[]{:S(2)}, u32[]{:S(2)}) %all-to-all-start) | async-done | bytes 786464 | tf_op jit(solution)/shard_map/all_to_all | solution.py:70
  46.2 1.4 gather_fusion.1
  48.0 0.8 copy.78
  49.1 33.5 %all-gather.2.cloned.1.call-done = bf16[96,16,1024]{2,0,1:T(8,128)(2,1)} async-done(((bf16[96,2,1024]{2,0,1:T(8,128)(2,1)}), bf16[96,16,1024]{2,0,1:T(8,128)(2,1)}) %all-gather.2.cloned.1.call-update) | async-done | bytes 3145744 | tf_op jit(solution)/shard_map/all_gather | solution.py:82
  82.6 3.6 %copy.79 = bf16[96,16,1024]{2,1,0:T(8,128)(2,1)S(1)} copy(bf16[96,16,1024]{2,0,1:T(8,128)(2,1)} %all-gather.2.cloned.1.call-done) | data formatting | bytes 6291456 | tf_op jit(solution)/shard_map/all_gather | solution.py:82
  86.2 3.8 %convolution_convert_fusion = bf16[1536,1024]{0,1:T(8,128)(2,1)S(1)} fusion(bf16[1536,1024]{1,0:T(8,128)(2,1)S(1)} %bitcast.78, bf16[1024,1024]{1,0:T(8,128)(2,1)S(1)} %copy-done), kind=kOutput, calls=%fused_computation.5 | convolution fusion | flops 3222798336 | bytes 8388608 | tf_op jit(solution)/shard_map/dot_general | solution.py:85
  90.1 1.2 convolution_convert_fusion.1
  91.3 1.2 convolution_convert_fusion.2
  92.5 2.1 pad_maximum_fusion
  94.5 6.3 %copy.80 = bf16[1536,1280]{1,0:T(8,128)(2,1)} copy(bf16[1536,1280]{0,1:T(8,128)(2,1)} %pad_maximum_fusion) | data formatting | bytes 7864320 | tf_op jit(solution)/shard_map/concatenate | solution.py:89
  100.9 0.6 copy-done.1
  101.5 0.6 gather_fusion.2
  102.1 0.6 gather_fusion.3
  103.5 53.5 %reduce-scatter.2.cloned.1.call-done = bf16[12,16,1280]{2,1,0:T(8,128)(2,1)} async-done(((bf16[96,16,1280]{2,1,0:T(8,128)(2,1)}), bf16[12,16,1280]{2,1,0:T(8,128)(2,1)}) %reduce-scatter.2.cloned.1.call-update) | async-done | bytes 491536 | tf_op jit(solution)/shard_map/reduce_scatter | solution.py:88
  157.0 1.1 slice.37
  158.7 0.5 fusion.40
  160.0 0.7 fusion
  161.1 1.0 fusion.1
  162.2 1.1 fusion.3
  163.2 0.7 fusion.12
  164.6 19.7 %all_to_all.28 = bf16[12,16,1024]{2,0,1:T(8,128)(2,1)S(1)} all-to-all(bf16[12,16,1024]{2,0,1:T(8,128)(2,1)S(1)} %copy.84), channel_id=1, replica_groups=mesh['grp'=8,'row'=8,'col'=8] {'row'}, dimensions={1} | all-to-all | bytes 786432 | tf_op jit(solution)/shard_map/all_to_all | solution.py:173
  185.1 1.7 copy.88
  186.7 12.2 %all-to-all-start.2 = ((bf16[64,3,2,1024]{3,2,1,0:T(2,128)(2,1)}), bf16[64,3,2,1024]{3,2,1,0:T(2,128)(2,1)S(1)}, u32[]{:S(2)}, u32[]{:S(2)}) async-start(bf16[64,3,2,1024]{3,2,1,0:T(2,128)(2,1)} %bitcast.24), calls=%async_computation.3 | async-start | bytes 1572864 | tf_op jit(solution)/shard_map/all_to_all | solution.py:181
  199.0 22.7 %all-to-all-done.2 = bf16[64,3,2,1024]{3,2,1,0:T(2,128)(2,1)S(1)} async-done(((bf16[64,3,2,1024]{3,2,1,0:T(2,128)(2,1)}), bf16[64,3,2,1024]{3,2,1,0:T(2,128)(2,1)S(1)}, u32[]{:S(2)}, u32[]{:S(2)}) %all-to-all-start.2) | async-done | bytes 786464 | tf_op jit(solution)/shard_map/all_to_all | solution.py:181
  221.7 0.6 fusion.13
  222.5 1.0 reshape.419
  (69 shorter events, 6.6 us)
Async XLA Ops:
  6.5 79.7 %copy-start = (bf16[1024,1024]{1,0:T(8,128)(2,1)S(1)}, bf16[1024,1024]{1,0:T(8,128)(2,1)}, u32[]{:S(2)}) copy-start(bf16[1024,1024]{1,0:T(8,128)(2,1)} %param.12) | copy-start | bytes 6291460
  9.3 14.2 %copy-start.7 = (s32[768]{0:T(1024)S(1)}, s32[768]{0:T(1024)}, u32[]{:S(2)}) copy-start(s32[768]{0:T(1024)} %param.17) | copy-start | bytes 9220
  11.8 34.4 %all-to-all-start = ((bf16[64,3,2,1024]{3,2,1,0:T(2,128)(2,1)}), bf16[64,3,2,1024]{3,2,1,0:T(2,128)(2,1)S(1)}, u32[]{:S(2)}, u32[]{:S(2)}) async-start(bf16[64,3,2,1024]{3,2,1,0:T(2,128)(2,1)} %copy.77), calls=%async_computation | async-start | bytes 1572864 | tf_op jit(solution)/shard_map/all_to_all | solution.py:70
  23.4 59.2 %all-gather.2.cloned.1.call-start = ((), (), s32[]{:S(2)}) async-start(), calls=%async_computation.4 | async-start | bytes 3538944 | tf_op jit(solution)/shard_map/all_gather | solution.py:82
  48.8 108.1 %reduce-scatter.2.cloned.1.call-start = ((), (), s32[]{:S(2)}) async-start(), calls=%async_computation.5 | async-start | bytes 4423680 | tf_op jit(solution)/shard_map/reduce_scatter | solution.py:88
  86.2 3.8 %copy-start.5 = (bf16[1024,128]{1,0:T(8,128)(2,1)S(1)}, bf16[1024,128]{1,0:T(8,128)(2,1)}, u32[]{:S(2)}) copy-start(bf16[1024,128]{1,0:T(8,128)(2,1)} %param.14) | copy-start | bytes 786436
  90.1 1.2 copy-start.6
  100.8 0.7 copy-start.1
  100.8 1.3 copy-start.2
  157.0 1.6 copy-start.3
  158.5 1.4 copy-start.4
  160.6 1.5 copy-start.8
  186.7 34.9 %all-to-all-start.2 = ((bf16[64,3,2,1024]{3,2,1,0:T(2,128)(2,1)}), bf16[64,3,2,1024]{3,2,1,0:T(2,128)(2,1)S(1)}, u32[]{:S(2)}, u32[]{:S(2)}) async-start(bf16[64,3,2,1024]{3,2,1,0:T(2,128)(2,1)} %bitcast.24), calls=%async_computation.3 | async-start | bytes 1572864 | tf_op jit(solution)/shard_map/all_to_all | solution.py:181
Sparse Core Ops, SparseCore 0:
  49.0 33.5 all-gather.1
  100.9 55.9 reduce-scatter.1
where the time goes:
time: 231 us; the launch traced here: 230 us
  waiting for transfers between devices  127 us (55%)
  local copies, waits for them, and re-layouts  24.5 us (11%)
  starting transfers between devices  24.1 us (10%)
  blocking collectives  19.7 us (9%)
  between operations  13.8 us (6%)
  other arithmetic  11.2 us (5%)
  matrix products  10.2 us (4%)
    reduce_scatter x1, waiting for transfers between devices, local(): lax.psum_scatter(jnp.concatenate([query_part, key_part, value_part], axis...  53.5 us
    all_gather x1, waiting for transfers between devices, local(): tokens = lax.all_gather(landed, 'col', axis=1, tiled=True)  33.5 us
    all_to_all x1, waiting for transfers between devices, local(): lax.all_to_all(returning.reshape(regions, capacity, slot_share, query_wid...  22.7 us
    all_to_all x1, blocking collectives, local(): lax.all_to_all(result, 'row', split_axis=1, concat_axis=0, tiled=True)  19.7 us
    all_to_all x1, waiting for transfers between devices, local(): lax.all_to_all(outgoing.reshape(regions, capacity, slot_width, feature_wi...  17.1 us
    all_to_all x1, starting transfers between devices, local(): lax.all_to_all(returning.reshape(regions, capacity, slot_share, query_wid...  12.2 us
    all_to_all x1, starting transfers between devices, local(): lax.all_to_all(outgoing.reshape(regions, capacity, slot_width, feature_wi...  11.6 us
    concatenate x1, local copies, waits for them, and re-layouts, local(): jnp.concatenate([query_part, key_part, value_part], axis=1)  6.26 us
  transfers between devices with their start and end apart: 4, of which 4 were waited for; matrix products, arithmetic and copies ran while one was open for 3% of the time, Pallas kernels for 0%

commit v1 on v0

--- a/solution.py
+++ b/solution.py
@@ -79,7 +79,24 @@
     landed = jnp.take(
         arrived.reshape(regions * capacity, slot_width, feature_width), source_row, axis=0
     )
-    tokens = lax.all_gather(landed, "col", axis=1, tiled=True)
+    peers, index, width = (lax.axis_size("col"), lax.axis_index("col"), landed.shape[1])
+    right = [(i, (i + 1) % peers) for i in range(peers)]
+    left = [(i, (i - 1) % peers) for i in range(peers)]
+    whole = jnp.zeros((*landed.shape[:1], peers * width, *landed.shape[1 + 1 :]), landed.dtype)
+    whole = lax.dynamic_update_slice_in_dim(whole, landed, index * width, axis=1)
+    from_left = from_right = landed
+    halfway = peers // 2
+    for step in range(1, halfway + 1):
+        from_left = lax.ppermute(from_left, "col", right)
+        whole = lax.dynamic_update_slice_in_dim(
+            whole, from_left, (index - step) % peers * width, axis=1
+        )
+        if step < peers - halfway:
+            from_right = lax.ppermute(from_right, "col", left)
+            whole = lax.dynamic_update_slice_in_dim(
+                whole, from_right, (index + step) % peers * width, axis=1
+            )
+    tokens = whole
     agents_here = cache_keys.shape[0]
     picked = tokens.reshape(lax.axis_size("row") * agents_here * slot_count, feature_width)
     query_part = jnp.dot(picked, query_weight, preferred_element_type=jnp.float32)

time: 231 us -> 236 us (1.022)
  waiting for transfers between devices: 127 us -> 108 us
  starting transfers between devices: 24.1 us -> 33.8 us
  local copies, waits for them, and re-layouts: 24.5 us -> 31.7 us
  matrix products: 10.2 us -> 15.9 us
    all_gather x1 -> x0, waiting for transfers between devices: 33.5 us -> none  [local(): tokens = lax.all_gather(landed, 'col', axis=1, tiled=True)]
    ppermute x0 -> x7, starting transfers between devices: none -> 10.1 us  [the longest x4 8.75 us: local(): from_left = lax.ppermute(from_left, 'col', right)]
    ppermute x0 -> x7, waiting for transfers between devices: none -> 9.85 us  [the longest x4 9.74 us: local(): from_left = lax.ppermute(from_left, 'col', right)]
    dynamic_update_slice x0 -> x7, local copies, waits for them, and re-layouts: none -> 9.56 us  [the longest x4 5.3 us: local(): lax.dynamic_update_slice_in_dim(whole, from_left, (index - step) % peers...]
    reduce_scatter x1, waiting for transfers between devices: 53.5 us -> 58.5 us  [local(): lax.psum_scatter(jnp.concatenate([query_part, key_part, value_part], axis...]
    all_gather x1 -> x0, local copies, waits for them, and re-layouts: 3.61 us -> none  [local(): tokens = lax.all_gather(landed, 'col', axis=1, tiled=True)]
  transfers between devices with their start and end apart: 4 -> 10, of which waited for: 4 -> 7; matrix products, arithmetic and copies ran while one was open for 3% -> 7% of each run, Pallas kernels for 0% -> 0%
where the time goes in v1:
time: 236 us; the launch traced here: 235 us
  waiting for transfers between devices  108 us (46%)
  starting transfers between devices  33.8 us (14%)
  local copies, waits for them, and re-layouts  31.7 us (13%)
  blocking collectives  19.7 us (8%)
  matrix products  15.9 us (7%)
  between operations  13.8 us (6%)
  other arithmetic  12.1 us (5%)
    reduce_scatter x1, waiting for transfers between devices, local(): lax.psum_scatter(jnp.concatenate([query_part, key_part, value_part], axis...  58.5 us
    all_to_all x1, waiting for transfers between devices, local(): lax.all_to_all(returning.reshape(regions, capacity, slot_share, query_wid...  22.7 us
    all_to_all x1, blocking collectives, local(): lax.all_to_all(result, 'row', split_axis=1, concat_axis=0, tiled=True)  19.7 us
    all_to_all x1, waiting for transfers between devices, local(): lax.all_to_all(outgoing.reshape(regions, capacity, slot_width, feature_wi...  17.1 us
    all_to_all x1, starting transfers between devices, local(): lax.all_to_all(returning.reshape(regions, capacity, slot_share, query_wid...  12.1 us
    all_to_all x1, starting transfers between devices, local(): lax.all_to_all(outgoing.reshape(regions, capacity, slot_width, feature_wi...  11.6 us
    ppermute x4, waiting for transfers between devices, local(): from_left = lax.ppermute(from_left, 'col', right)  9.74 us
    ppermute x4, starting transfers between devices, local(): from_left = lax.ppermute(from_left, 'col', right)  8.75 us
  transfers between devices with their start and end apart: 10, of which 7 were waited for; matrix products, arithmetic and copies ran while one was open for 7% of the time, Pallas kernels for 0%

profile of v1, /device:TPU:1, one launch (start us, length us, event | category | flops | bytes accessed | tf_op | source)
XLA Modules:
  0.0 235.3 jit_solution(7905800962975157471)
XLA Ops:
  8.1 1.2 copy.75
  10.1 1.7 copy.59
  11.8 11.6 %all-to-all-start = ((bf16[64,3,2,1024]{3,2,1,0:T(2,128)(2,1)}), bf16[64,3,2,1024]{3,2,1,0:T(2,128)(2,1)S(1)}, u32[]{:S(2)}, u32[]{:S(2)}) async-start(bf16[64,3,2,1024]{3,2,1,0:T(2,128)(2,1)} %copy.59), calls=%async_computation | async-start | bytes 1572864 | tf_op jit(solution)/shard_map/all_to_all | solution.py:70
  23.5 4.4 %sort.17 = (s32[768]{0:T(1024)}, s32[768]{0:T(1024)S(1)}) sort(s32[768]{0:T(1024)S(1)} %copy-done.8, s32[768]{0:T(1024)S(1)} %iota.103), dimensions={0}, to_apply=%region_0.1 | sort | flops 7680 | bytes 12288 | tf_op jit(solution)/shard_map/jit(argsort)/sort | solution.py:58
  29.0 17.1 %all-to-all-done = bf16[64,3,2,1024]{3,2,1,0:T(2,128)(2,1)S(1)} async-done(((bf16[64,3,2,1024]{3,2,1,0:T(2,128)(2,1)}), bf16[64,3,2,1024]{3,2,1,0:T(2,128)(2,1)S(1)}, u32[]{:S(2)}, u32[]{:S(2)}) %all-to-all-start) | async-done | bytes 786464 | tf_op jit(solution)/shard_map/all_to_all | solution.py:70
  46.2 1.4 gather_fusion.1
  47.5 2.0 broadcast_in_dim.101
  49.6 1.3 constant_dynamic-update-slice_fusion.7
  50.9 2.1 collective-permute-start
  53.0 4.7 %collective-permute-done = bf16[96,2,1024]{2,1,0:T(2,128)(2,1)S(1)} collective-permute-done((bf16[96,2,1024]{2,1,0:T(2,128)(2,1)S(1)}, bf16[96,2,1024]{2,1,0:T(2,128)(2,1)S(1)}, u32[]{:S(2)}, u32[]{:S(2)}) %collective-permute-start) | collective-permute-done | bytes 393248 | tf_op jit(solution)/shard_map/ppermute | solution.py:90
  57.7 2.5 %collective-permute-start.2 = (bf16[96,2,1024]{2,1,0:T(2,128)(2,1)S(1)}, bf16[96,2,1024]{2,1,0:T(2,128)(2,1)S(1)}, u32[]{:S(2)}, u32[]{:S(2)}) collective-permute-start(bf16[96,2,1024]{2,1,0:T(2,128)(2,1)S(1)} %collective-permute-done), channel_id=1, source_target_pairs={{0,1},{1,2},{2,3},{3,4},{4,5},{5,6},{6,7},{7,0},{8,9},{9,10},{10,1... | collective-permute-start | bytes 1179656 | tf_op jit(solution)/shard_map/ppermute | solution.py:90
  60.3 4.6 %collective-permute-done.2 = bf16[96,2,1024]{2,1,0:T(2,128)(2,1)S(1)} collective-permute-done((bf16[96,2,1024]{2,1,0:T(2,128)(2,1)S(1)}, bf16[96,2,1024]{2,1,0:T(2,128)(2,1)S(1)}, u32[]{:S(2)}, u32[]{:S(2)}) %collective-permute-start.2) | collective-permute-done | bytes 393248 | tf_op jit(solution)/shard_map/ppermute | solution.py:90
  64.9 2.5 %collective-permute-start.4 = (bf16[96,2,1024]{2,1,0:T(2,128)(2,1)S(1)}, bf16[96,2,1024]{2,1,0:T(2,128)(2,1)S(1)}, u32[]{:S(2)}, u32[]{:S(2)}) collective-permute-start(bf16[96,2,1024]{2,1,0:T(2,128)(2,1)S(1)} %collective-permute-done.2), channel_id=1, source_target_pairs={{0,1},{1,2},{2,3},{3,4},{4,5},{5,6},{6,7},{7,0},{8,9},{9,10},{10,1... | collective-permute-start | bytes 1179656 | tf_op jit(solution)/shard_map/ppermute | solution.py:90
  67.4 2.1 constant_dynamic-update-slice_fusion.6
  69.5 1.3 collective-permute-start.5
  70.8 2.1 constant_dynamic-update-slice_fusion.5
  72.9 1.7 collective-permute-start.6
  74.6 1.1 constant_dynamic-update-slice_fusion.4
  75.7 1.1 constant_dynamic-update-slice_fusion.3
  76.8 1.1 constant_dynamic-update-slice_fusion.2
  79.3 1.1 constant_dynamic-update-slice_fusion
  80.4 5.7 %convolution_convert_fusion = bf16[1536,1024]{0,1:T(8,128)(2,1)S(1)} fusion(bf16[1536,1024]{1,0:T(8,128)(2,1)} %bitcast.8, bf16[1024,1024]{1,0:T(8,128)(2,1)S(1)} %copy-done), kind=kOutput, calls=%fused_computation.5 | convolution fusion | flops 3222798336 | bytes 8388608 | tf_op jit(solution)/shard_map/dot_general | solution.py:102
  86.1 3.1 %convolution_convert_fusion.1 = bf16[1536,128]{0,1:T(8,128)(2,1)S(1)} fusion(bf16[1536,1024]{1,0:T(8,128)(2,1)} %bitcast.8, bf16[1024,128]{1,0:T(8,128)(2,1)S(1)} %copy-done.6), kind=kOutput, calls=%fused_computation.9 | convolution fusion | flops 402849792 | bytes 3801088 | tf_op jit(solution)/shard_map/dot_general | solution.py:104
  89.2 3.1 %convolution_convert_fusion.2 = bf16[1536,128]{0,1:T(8,128)(2,1)S(1)} fusion(bf16[1536,1024]{1,0:T(8,128)(2,1)} %bitcast.8, bf16[1024,128]{1,0:T(8,128)(2,1)S(1)} %copy-done.7), kind=kOutput, calls=%fused_computation.10 | convolution fusion | flops 402849792 | bytes 3801088 | tf_op jit(solution)/shard_map/dot_general | solution.py:103
  92.3 2.1 pad_maximum_fusion
  94.4 6.3 %copy.60 = bf16[1536,1280]{1,0:T(8,128)(2,1)} copy(bf16[1536,1280]{0,1:T(8,128)(2,1)} %pad_maximum_fusion) | data formatting | bytes 7864320 | tf_op jit(solution)/shard_map/concatenate | solution.py:106
  103.4 58.5 %reduce-scatter.2.cloned.1.call-done = bf16[12,16,1280]{2,1,0:T(8,128)(2,1)} async-done(((bf16[96,16,1280]{2,1,0:T(8,128)(2,1)}), bf16[12,16,1280]{2,1,0:T(8,128)(2,1)}) %reduce-scatter.2.cloned.1.call-update) | async-done | bytes 491536 | tf_op jit(solution)/shard_map/reduce_scatter | solution.py:105
  162.0 1.1 slice.37
  169.6 19.7 %all_to_all.28 = bf16[12,16,1024]{2,0,1:T(8,128)(2,1)S(1)} all-to-all(bf16[12,16,1024]{2,0,1:T(8,128)(2,1)S(1)} %copy.64), channel_id=1, replica_groups=mesh['grp'=8,'row'=8,'col'=8] {'row'}, dimensions={1} | all-to-all | bytes 786432 | tf_op jit(solution)/shard_map/all_to_all | solution.py:190
  190.1 1.7 copy.68
  191.8 12.1 %all-to-all-start.2 = ((bf16[64,3,2,1024]{3,2,1,0:T(2,128)(2,1)}), bf16[64,3,2,1024]{3,2,1,0:T(2,128)(2,1)S(1)}, u32[]{:S(2)}, u32[]{:S(2)}) async-start(bf16[64,3,2,1024]{3,2,1,0:T(2,128)(2,1)} %bitcast.24), calls=%async_computation.3 | async-start | bytes 1572864 | tf_op jit(solution)/shard_map/all_to_all | solution.py:198
  203.9 22.7 %all-to-all-done.2 = bf16[64,3,2,1024]{3,2,1,0:T(2,128)(2,1)S(1)} async-done(((bf16[64,3,2,1024]{3,2,1,0:T(2,128)(2,1)}), bf16[64,3,2,1024]{3,2,1,0:T(2,128)(2,1)S(1)}, u32[]{:S(2)}, u32[]{:S(2)}) %all-to-all-start.2) | async-done | bytes 786464 | tf_op jit(solution)/shard_map/all_to_all | solution.py:198
  (88 shorter events, 16.7 us)
Async XLA Ops:
  6.5 73.9 %copy-start = (bf16[1024,1024]{1,0:T(8,128)(2,1)S(1)}, bf16[1024,1024]{1,0:T(8,128)(2,1)}, u32[]{:S(2)}) copy-start(bf16[1024,1024]{1,0:T(8,128)(2,1)} %param.12) | copy-start | bytes 6291460
  9.3 14.2 %copy-start.8 = (s32[768]{0:T(1024)S(1)}, s32[768]{0:T(1024)}, u32[]{:S(2)}) copy-start(s32[768]{0:T(1024)} %param.17) | copy-start | bytes 9220
  11.8 34.4 %all-to-all-start = ((bf16[64,3,2,1024]{3,2,1,0:T(2,128)(2,1)}), bf16[64,3,2,1024]{3,2,1,0:T(2,128)(2,1)S(1)}, u32[]{:S(2)}, u32[]{:S(2)}) async-start(bf16[64,3,2,1024]{3,2,1,0:T(2,128)(2,1)} %copy.59), calls=%async_computation | async-start | bytes 1572864 | tf_op jit(solution)/shard_map/all_to_all | solution.py:70
  23.4 138.5 %reduce-scatter.2.cloned.1.call-start = ((), (), s32[]{:S(2)}) async-start(), calls=%async_computation.4 | async-start | bytes 4423680 | tf_op jit(solution)/shard_map/reduce_scatter | solution.py:105
  50.9 6.8 %collective-permute-start = (bf16[96,2,1024]{2,1,0:T(2,128)(2,1)S(1)}, bf16[96,2,1024]{2,1,0:T(2,128)(2,1)S(1)}, u32[]{:S(2)}, u32[]{:S(2)}) collective-permute-start(bf16[96,2,1024]{2,1,0:T(2,128)(2,1)S(1)} %get-tuple-element.9), channel_id=1, source_target_pairs={{0,1},{1,2},{2,3},{3,4},{4,5},{5,6},{6,7},{7,0},{8,9},{9,10},{10,1... | collective-permute-start | bytes 1179656 | tf_op jit(solution)/shard_map/ppermute | solution.py:90
  53.0 7.3 %collective-permute-start.1 = (bf16[96,2,1024]{2,1,0:T(2,128)(2,1)S(1)}, bf16[96,2,1024]{2,1,0:T(2,128)(2,1)}, u32[]{:S(2)}, u32[]{:S(2)}) collective-permute-start(bf16[96,2,1024]{2,1,0:T(2,128)(2,1)S(1)} %get-tuple-element.9), channel_id=1, source_target_pairs={{0,7},{1,0},{2,1},{3,2},{4,3},{5,4},{6,5},{7,6},{8,15},{9,8},{10,9... | collective-permute-start | bytes 1179656 | tf_op jit(solution)/shard_map/ppermute | solution.py:95
  57.7 7.2 %copy-start.5 = (bf16[96,2,1024]{2,1,0:T(2,128)(2,1)}, bf16[96,2,1024]{2,1,0:T(2,128)(2,1)S(1)}, u32[]{:S(2)}) copy-start(bf16[96,2,1024]{2,1,0:T(2,128)(2,1)S(1)} %collective-permute-done) | copy-start | bytes 1179652
  57.7 7.2 %collective-permute-start.2 = (bf16[96,2,1024]{2,1,0:T(2,128)(2,1)S(1)}, bf16[96,2,1024]{2,1,0:T(2,128)(2,1)S(1)}, u32[]{:S(2)}, u32[]{:S(2)}) collective-permute-start(bf16[96,2,1024]{2,1,0:T(2,128)(2,1)S(1)} %collective-permute-done), channel_id=1, source_target_pairs={{0,1},{1,2},{2,3},{3,4},{4,5},{5,6},{6,7},{7,0},{8,9},{9,10},{10,1... | collective-permute-start | bytes 1179656 | tf_op jit(solution)/shard_map/ppermute | solution.py:90
  60.3 9.2 %collective-permute-start.3 = (bf16[96,2,1024]{2,1,0:T(2,128)(2,1)}, bf16[96,2,1024]{2,1,0:T(2,128)(2,1)S(1)}, u32[]{:S(2)}, u32[]{:S(2)}) collective-permute-start(bf16[96,2,1024]{2,1,0:T(2,128)(2,1)} %collective-permute-done.1), channel_id=1, source_target_pairs={{0,7},{1,0},{2,1},{3,2},{4,3},{5,4},{6,5},{7,6},{8,15},{9,8},{10,9... | collective-permute-start | bytes 1179656 | tf_op jit(solution)/shard_map/ppermute | solution.py:95
  64.9 8.0 %collective-permute-start.4 = (bf16[96,2,1024]{2,1,0:T(2,128)(2,1)S(1)}, bf16[96,2,1024]{2,1,0:T(2,128)(2,1)S(1)}, u32[]{:S(2)}, u32[]{:S(2)}) collective-permute-start(bf16[96,2,1024]{2,1,0:T(2,128)(2,1)S(1)} %collective-permute-done.2), channel_id=1, source_target_pairs={{0,1},{1,2},{2,3},{3,4},{4,5},{5,6},{6,7},{7,0},{8,9},{9,10},{10,1... | collective-permute-start | bytes 1179656 | tf_op jit(solution)/shard_map/ppermute | solution.py:90
  69.5 8.3 %collective-permute-start.5 = (bf16[96,2,1024]{2,1,0:T(2,128)(2,1)S(1)}, bf16[96,2,1024]{2,1,0:T(2,128)(2,1)S(1)}, u32[]{:S(2)}, u32[]{:S(2)}) collective-permute-start(bf16[96,2,1024]{2,1,0:T(2,128)(2,1)S(1)} %collective-permute-done.3), channel_id=1, source_target_pairs={{0,7},{1,0},{2,1},{3,2},{4,3},{5,4},{6,5},{7,6},{8,15},{9,8},{10,9... | collective-permute-start | bytes 1179656 | tf_op jit(solution)/shard_map/ppermute | solution.py:95
  72.9 6.4 %collective-permute-start.6 = (bf16[96,2,1024]{2,1,0:T(2,128)(2,1)S(1)}, bf16[96,2,1024]{2,1,0:T(2,128)(2,1)S(1)}, u32[]{:S(2)}, u32[]{:S(2)}) collective-permute-start(bf16[96,2,1024]{2,1,0:T(2,128)(2,1)S(1)} %collective-permute-done.4), channel_id=1, source_target_pairs={{0,1},{1,2},{2,3},{3,4},{4,5},{5,6},{6,7},{7,0},{8,9},{9,10},{10,1... | collective-permute-start | bytes 1179656 | tf_op jit(solution)/shard_map/ppermute | solution.py:90
  80.4 5.7 %copy-start.6 = (bf16[1024,128]{1,0:T(8,128)(2,1)S(1)}, bf16[1024,128]{1,0:T(8,128)(2,1)}, u32[]{:S(2)}) copy-start(bf16[1024,128]{1,0:T(8,128)(2,1)} %param.14) | copy-start | bytes 786436
  86.1 3.1 %copy-start.7 = (bf16[1024,128]{1,0:T(8,128)(2,1)S(1)}, bf16[1024,128]{1,0:T(8,128)(2,1)}, u32[]{:S(2)}) copy-start(bf16[1024,128]{1,0:T(8,128)(2,1)} %param.13) | copy-start | bytes 786436
  100.7 0.7 copy-start.1
  100.7 1.3 copy-start.2
  161.9 1.6 copy-start.3
  163.5 1.4 copy-start.4
  165.6 1.5 copy-start.9
  191.8 34.9 %all-to-all-start.2 = ((bf16[64,3,2,1024]{3,2,1,0:T(2,128)(2,1)}), bf16[64,3,2,1024]{3,2,1,0:T(2,128)(2,1)S(1)}, u32[]{:S(2)}, u32[]{:S(2)}) async-start(bf16[64,3,2,1024]{3,2,1,0:T(2,128)(2,1)} %bitcast.24), calls=%async_computation.3 | async-start | bytes 1572864 | tf_op jit(solution)/shard_map/all_to_all | solution.py:198
Sparse Core Ops, SparseCore 0:
  100.9 61.0 reduce-scatter.1
